TPU v7x, 256 devices: a whole 4x4x8 slice. The times are simulated.
256 devices in a mesh: ctx: 64 (over z, x, core), dp: 4 (over y).
Axes of the slice: x: 4, y: 4, z: 8, core: 2. Of those that a mesh axis runs over, the one named last changes fastest.
Arguments:
- query_in: bfloat16 [4, 16384, 4096], P('dp', 'ctx'), may hold values from -6 to 6
- key_in: bfloat16 [4, 16384, 512], P('dp', 'ctx'), may hold values from -6 to 6
- value_rows_input: bfloat16 [4, 16384, 512], P('dp', 'ctx'), may hold values from -6 to 6
- grad_out: bfloat16 [4, 16384, 4096], P('dp', 'ctx'), may hold values from -12 to 12
- query_bias: float32 [4096], replicated, may hold values from -1.5 to 1.5
- key_blocks: int32 [4, 128, 6], P('dp'), may hold values from -1 to 127, as said below
- trace_len: int32 [4], P('dp'), may hold values from 8192 to 16384, as said below
Outputs:
- grad_query: bfloat16 [4, 16384, 4096], P('dp', 'ctx')
- grad_key: bfloat16 [4, 16384, 512], P('dp', 'ctx')
- grad_value: bfloat16 [4, 16384, 512], P('dp', 'ctx')
- bias_grad: float32 [4096], replicated
Inputs may be any that keep to these rules, and one draw needn't show every extreme that they name: `key_blocks`: blocks are numbered by position. Entry 2 + d of query block q's list is q - d or -1, and entry 2 is always q; entry r < 2 is r or -1, and -1 whenever r >= q - 3. `trace_len`: some trace has 16384 tokens and some 16384 // 2.
All inputs are finite; a program needn't handle non-finite values.
Results may differ from a plain program's by a relative error of at most 0.011.
The roundings to bfloat16 on the way count: a program that leaves them out, or rounds other values in their place, can miss the bound.
Values may be sent and summed in bfloat16 or wider, within the bound.
A program may use at most 128 MiB of HBM per device.

v0:
```python
import math
import jax
import jax.numpy as jnp
from jax import lax
from jax.sharding import PartitionSpec as P

HEAD_SIZE = 128
BLOCK = 128
PROMPT = 2
WINDOW = 3


def from_behind(value, axis, steps):
    count = lax.axis_size(axis)
    initial, last = (max(0, -steps), min(count, count - steps))
    return lax.ppermute(value, axis, [(source, source + steps) for source in range(initial, last)])


def broadcast(value, axis, source):
    kept = jnp.where(lax.axis_index(axis) == source, value, 0).astype(value.dtype)
    return lax.psum(kept, axis)


def attend(queries, cand_keys, cand_vals, grad_rows, allowed):
    score_scale = HEAD_SIZE ** (-0.5)
    scores = score_scale * jnp.einsum(
        "tqkgd,tskd->tkgqs", queries, cand_keys, preferred_element_type=jnp.float32
    )
    mask_full = allowed[:, None, None]
    scores = jnp.where(mask_full, scores, -1e30)
    row_max = jnp.max(scores, axis=-1, keepdims=True)
    probs = jnp.where(mask_full, jnp.exp(scores - row_max), 0.0)
    totals = jnp.sum(probs, axis=-1, keepdims=True)
    row_live = jnp.any(allowed, axis=-1)[:, None, None, :, None]
    probs = probs / jnp.where(row_live, totals, 1.0)
    probs_low = probs.astype(jnp.bfloat16)
    attended = jnp.einsum(
        "tkgqs,tskd->tqkgd", probs_low, cand_vals, preferred_element_type=jnp.float32
    )
    row_dot = jnp.sum(grad_rows * attended, axis=-1).transpose(0, 2, 3, 1)[..., None]
    grad_probs = jnp.einsum(
        "tqkgd,tskd->tkgqs", grad_rows, cand_vals, preferred_element_type=jnp.float32
    )
    grad_scores = (probs * (grad_probs - row_dot)).astype(jnp.bfloat16)
    grad_query = score_scale * jnp.einsum(
        "tkgqs,tskd->tqkgd", grad_scores, cand_keys, preferred_element_type=jnp.float32
    )
    grad_key = score_scale * jnp.einsum(
        "tkgqs,tqkgd->tskd", grad_scores, queries, preferred_element_type=jnp.float32
    )
    grad_value = jnp.einsum(
        "tkgqs,tqkgd->tskd", probs_low, grad_rows, preferred_element_type=jnp.float32
    )
    return (grad_query, grad_key, grad_value)


def body(query_in, key_in, value_rows_input, grad_out, query_bias, key_blocks, trace_len):
    ctx_count = lax.axis_size("ctx")
    rank_ctx = lax.axis_index("ctx")
    traces = query_in.shape[0]
    width_kv = key_in.shape[-1]
    width_q = query_in.shape[-1]
    heads_kv = width_kv // HEAD_SIZE
    group_size = width_q // width_kv
    cand_count = PROMPT + WINDOW + 1
    kv_pair = jnp.concatenate([key_in, value_rows_input], axis=-1).reshape(
        traces, 2, BLOCK, 2 * width_kv
    )
    own_ids = jnp.stack([rank_ctx, 2 * ctx_count - 1 - rank_ctx])
    half_count = kv_pair.shape[1]
    from_lower = jnp.stack([from_behind(kv_pair, "ctx", offset) for offset in range(1, WINDOW + 1)])
    from_upper = jnp.stack(
        [from_behind(kv_pair, "ctx", -offset) for offset in range(1, WINDOW + 1)]
    )
    offsets = jnp.arange(1, WINDOW + 1, dtype=jnp.int32)
    lower_dev = rank_ctx - offsets
    upper_dev = rank_ctx + offsets
    lower_ids = jnp.stack([lower_dev, 2 * ctx_count - 1 - lower_dev], axis=1)
    upper_ids = jnp.stack([upper_dev, 2 * ctx_count - 1 - upper_dev], axis=1)
    lower_ids = jnp.where((lower_dev >= 0)[:, None], lower_ids, -1000).reshape(-1)
    upper_ids = jnp.where((upper_dev < ctx_count)[:, None], upper_ids, -1000).reshape(-1)
    lower_data = from_lower.transpose(1, 0, 2, 3, 4).reshape(
        traces, WINDOW * half_count, BLOCK, 2 * width_kv
    )
    upper_data = from_upper.transpose(1, 0, 2, 3, 4).reshape(
        traces, WINDOW * half_count, BLOCK, 2 * width_kv
    )
    data_list = [kv_pair, lower_data, upper_data]
    id_list = [own_ids, lower_ids, upper_ids]
    slot_data = jnp.concatenate(data_list, axis=1)
    slot_ids = jnp.concatenate(id_list)
    targets = own_ids[:, None] - jnp.arange(WINDOW + 1, dtype=jnp.int32)[None]
    chooser = (slot_ids[None, None, :] == targets[..., None]).astype(jnp.bfloat16)
    window_kv = jnp.einsum(
        "jdn,tnbf->tjdbf", chooser, slot_data, preferred_element_type=jnp.float32
    ).astype(jnp.bfloat16)
    first_half = kv_pair[:, 0]
    prompt_kv = jnp.stack(
        [broadcast(first_half, "ctx", source) for source in range(PROMPT)], axis=1
    )
    block_rows = jnp.take(key_blocks, own_ids, axis=1)
    queries = (
        (query_in.astype(jnp.float32) + query_bias)
        .astype(jnp.bfloat16)
        .reshape(traces, 2, BLOCK, heads_kv, group_size, HEAD_SIZE)
    )
    grad_rows = grad_out.reshape(traces, 2, BLOCK, heads_kv, group_size, HEAD_SIZE)
    prompt_grad = jnp.zeros((traces, PROMPT, BLOCK, 2 * width_kv), jnp.float32)
    slot_grad = jnp.zeros((traces, slot_data.shape[1], BLOCK, 2 * width_kv), jnp.float32)
    query_parts = []
    for half_idx in range(2):
        block_here = own_ids[half_idx]
        candidates = jnp.concatenate([prompt_kv, window_kv[:, half_idx]], axis=1)
        cand_keys = candidates[..., :width_kv].reshape(
            traces, cand_count * BLOCK, heads_kv, HEAD_SIZE
        )
        cand_vals = candidates[..., width_kv:].reshape(
            traces, cand_count * BLOCK, heads_kv, HEAD_SIZE
        )
        key_ids = jnp.concatenate(
            [
                jnp.arange(PROMPT, dtype=jnp.int32),
                block_here - jnp.arange(WINDOW + 1, dtype=jnp.int32),
            ]
        )
        prompt_ok = jnp.concatenate(
            [
                jnp.arange(PROMPT, dtype=jnp.int32) < block_here - WINDOW,
                jnp.ones((WINDOW + 1,), jnp.bool_),
            ]
        )
        block_ok = (block_rows[:, half_idx] >= 0) & prompt_ok[None]
        key_pos = (key_ids[:, None] * BLOCK + jnp.arange(BLOCK, dtype=jnp.int32)[None]).reshape(-1)
        query_pos = block_here * BLOCK + jnp.arange(BLOCK, dtype=jnp.int32)
        length = trace_len[:, None, None]
        allowed = (
            jnp.repeat(block_ok, BLOCK, axis=1)[:, None, :]
            & (key_pos[None, None, :] <= query_pos[None, :, None])
            & (key_pos[None, None, :] < length)
            & (query_pos[None, :, None] < length)
        )
        grad_query, grad_key, grad_value = attend(
            queries[:, half_idx], cand_keys, cand_vals, grad_rows[:, half_idx], allowed
        )
        query_parts.append(grad_query)
        contrib = jnp.concatenate(
            [
                grad_key.reshape(traces, cand_count, BLOCK, width_kv),
                grad_value.reshape(traces, cand_count, BLOCK, width_kv),
            ],
            axis=-1,
        )
        prompt_grad = prompt_grad + contrib[:, :PROMPT]
        slot_grad = slot_grad + jnp.einsum(
            "dn,tdbf->tnbf",
            chooser[half_idx].astype(jnp.float32),
            contrib[:, PROMPT:],
            precision=lax.Precision.HIGHEST,
        )
    span = WINDOW * half_count
    own_grad = slot_grad[:, 0:2]
    lower_grad = (
        slot_grad[:, 2 : 2 + span]
        .reshape(traces, WINDOW, half_count, BLOCK, 2 * width_kv)
        .transpose(1, 0, 2, 3, 4)
    )
    upper_grad = (
        slot_grad[:, 2 + span : 2 + 2 * span]
        .reshape(traces, WINDOW, half_count, BLOCK, 2 * width_kv)
        .transpose(1, 0, 2, 3, 4)
    )
    low_part = jnp.zeros_like(lower_grad[0])
    up_part = jnp.zeros_like(upper_grad[0])
    for offset in range(1, WINDOW + 1):
        low_part = low_part + from_behind(lower_grad[offset - 1], "ctx", -offset)
        up_part = up_part + from_behind(upper_grad[offset - 1], "ctx", offset)
    kv_grad = own_grad + low_part + up_part
    owners = jnp.arange(PROMPT, dtype=jnp.int32)
    query_all = jnp.stack(query_parts, axis=1)
    local_bias = jnp.sum(query_all, axis=(0, 1, 2)).reshape(width_q)
    shared_total = lax.psum(prompt_grad, "ctx")
    bias_total = lax.psum(local_bias, ("ctx", "dp"))
    owned = (owners == rank_ctx).astype(jnp.float32)
    kv_grad = kv_grad.at[:, 0].add(jnp.sum(owned[None, :, None, None] * shared_total, axis=1))
    grad_query_out = query_all.reshape(traces, 2 * BLOCK, width_q).astype(jnp.bfloat16)
    grad_key_out = kv_grad[..., :width_kv].reshape(traces, 2 * BLOCK, width_kv).astype(jnp.bfloat16)
    grad_value_out = (
        kv_grad[..., width_kv:].reshape(traces, 2 * BLOCK, width_kv).astype(jnp.bfloat16)
    )
    all_traces = traces * lax.axis_size("dp")
    bias_out = bias_total / math.sqrt(all_traces * 2 * BLOCK * ctx_count)
    return (grad_query_out, grad_key_out, grad_value_out, bias_out)


def solution(mesh):
    return jax.shard_map(
        body,
        mesh=mesh,
        in_specs=(
            P("dp", "ctx", None),
            P("dp", "ctx", None),
            P("dp", "ctx", None),
            P("dp", "ctx", None),
            P(),
            P("dp", None, None),
            P("dp"),
        ),
        out_specs=(P("dp", "ctx", None), P("dp", "ctx", None), P("dp", "ctx", None), P()),
        check_vma=False,
    )
```

profile of v0, /device:TPU:2, one launch (start us, length us, event | category | flops | bytes accessed | tf_op | source)
XLA Modules:
  0.0 588.3 jit_solution(5824512596889643687)
XLA Ops:
  9.7 4.2 collective-permute-start.4
  15.9 4.8 collective-permute-start.2
  35.2 2.9 fusion.73
  38.3 3.7 collective-permute-start
  42.5 3.3 fusion.74
  48.9 4.4 collective-permute-done
  55.6 2.7 convert_bitcast_fusion
  60.0 162.5 %all-reduce.8.cloned.1.call-done = (bf16[1,1,128,1024]{3,1,2,0:T(2,128)(2,1)}, bf16[1,1,128,1024]{3,1,2,0:T(2,128)(2,1)}) async-done(((bf16[1,1,128,1024]{3,1,2,0:T(2,128)(2,1)}, bf16[1,1,128,1024]{3,1,2,0:T(2,128)(2,1)}), (bf16[1,1,128,1024]{3,1,2,0:T(2,128)(2,1)}, bf16[1,1,128,1024]{3,1,2,0:T(2,128)(2,1)})) %all-reduce.8.cloned.1.call-update) | async-done | bytes 524304 | tf_op jit(solution)/shard_map/psum | solution.py:21
  222.5 4.6 pad_maximum_fusion
  233.5 2.7 fusion.75
  248.8 3.2 fusion.9
  252.0 5.3 fusion.40
  257.4 5.2 fusion.29
  262.6 7.1 %fusion.11 = bf16[4,8,128,768]{2,3,1,0:T(8,128)(2,1)S(1)} fusion(f32[4,8,128]{2,1,0:T(8,128)S(1)} %bitcast.338, f32[4,8,128]{2,1,0:T(8,128)S(1)} %broadcast_select_fusion.2, f32[4,8,128]{2,1,0:T(8,128)S(1)} %get-tuple-element.46, f32[4,768,128,8]{2,1,3,0:T(8,128)S(1)} %get-tuple-element.47, pred[128,768]{0,1:T(8,128)(4,1)S(1)} %and_and_fusion, ...), kind=kOutput, calls=%fused_computation.19 | convolution fusion | flops 830472192 | bytes 20856832 | tf_op jit(solution)/shard_map/tqkgd,tskd->tkgqs/dot_general | solution.py:41
  272.8 3.4 fusion.35
  276.2 2.8 copy.106
  279.0 3.7 copy_dynamic-update-slice_fusion.1
  285.1 3.2 fusion.7
  288.4 4.8 fusion.37
  293.2 5.2 fusion.30
  298.4 7.3 %fusion.10 = bf16[4,8,128,768]{2,3,1,0:T(8,128)(2,1)S(1)} fusion(f32[4,8,128]{2,1,0:T(8,128)S(1)} %bitcast.339, f32[4,8,128]{2,1,0:T(8,128)S(1)} %broadcast_select_fusion.3, f32[4,8,128]{2,1,0:T(8,128)S(1)} %get-tuple-element.48, f32[4,768,128,8]{2,1,3,0:T(8,128)S(1)} %get-tuple-element.49, pred[128,768]{0,1:T(8,128)(4,1)S(1)} %and_and_fusion.1, ...), kind=kOutput, calls=%fused_computation.18 | convolution fusion | flops 830472192 | bytes 20856832 | tf_op jit(solution)/shard_map/tqkgd,tskd->tkgqs/dot_general | solution.py:41
  308.8 3.4 fusion.36
  318.2 6.9 %fusion.28 = f32[128,1024,14]{1,2,0:T(8,128)} fusion(f32[1,6,128,1024]{3,1,2,0:T(8,128)S(1)} %copy_dynamic-update-slice_fusion.2, pred[2,4,14]{2,1,0:T(4,128)(4,1)S(1)} %copy-done.26), kind=kOutput, calls=%fused_computation.40 | convolution fusion | flops 88080384 | bytes 9437696 | tf_op jit(solution)/shard_map/dn,tdbf->tnbf/dot_general | solution.py:154
  330.1 10.6 %add_bitcast_fusion = f32[1,14,128,1024]{3,1,2,0:T(8,128)S(1)} fusion(f32[128,1024,14]{1,2,0:T(8,128)} %fusion.28, f32[1,6,128,1024]{3,1,2,0:T(8,128)} %copy-done.4, pred[2,4,14]{2,1,0:T(4,128)(4,1)S(1)} %copy-done.26), kind=kOutput, calls=%fused_computation.17 | convolution fusion | flops 89915392 | bytes 17826304 | tf_op jit(solution)/shard_map/dn,tdbf->tnbf/dot_general | solution.py:154
  340.8 3.6 fusion.71
  350.4 3.0 collective-permute-start.10
  353.4 4.5 collective-permute-start.9
  365.1 23.8 %collective-permute-done.7 = f32[1,2,128,1024]{3,1,2,0:T(2,128)S(1)} collective-permute-done((f32[1,2,128,1024]{3,1,2,0:T(2,128)S(1)}, f32[1,2,128,1024]{3,1,2,0:T(2,128)S(1)}, u32[]{:S(2)}, u32[]{:S(2)}) %collective-permute-start.7) | collective-permute-done | bytes 1048608 | tf_op jit(solution)/shard_map/ppermute | solution.py:16
  395.0 95.3 %psum.31 = f32[4096]{0:T(1024)S(1)} all-reduce(f32[4096]{0:T(1024)S(1)} %add_bitcast_fusion.1), channel_id=1, replica_groups=mesh['ctx'=64,'dp'=4] {'ctx','dp'}, use_global_device_ids=true, to_apply=%region_14.15 | all-reduce | flops 4096 | bytes 32768 | tf_op jit(solution)/shard_map/psum | solution.py:182
  490.9 75.6 %all-reduce.6.cloned.1.call-done = f32[1,2,128,1024]{3,1,2,0:T(2,128)} async-done(((f32[1,2,128,1024]{3,1,2,0:T(2,128)}), f32[1,2,128,1024]{3,1,2,0:T(2,128)}) %all-reduce.6.cloned.1.call-update) | async-done | bytes 1048592 | tf_op jit(solution)/shard_map/psum | solution.py:181
  569.2 5.6 fusion.45
  575.4 3.7 scatter-add.4
  (170 shorter events, 89.5 us)
Async XLA Ops:
  7.2 20.2 %copy-start.13 = (bf16[1,256,4096]{2,1,0:T(8,128)(2,1)S(1)}, bf16[1,256,4096]{2,1,0:T(8,128)(2,1)}, u32[]{:S(2)}) copy-start(bf16[1,256,4096]{2,1,0:T(8,128)(2,1)} %param.9) | copy-start | bytes 6291460
  7.2 215.4 %all-reduce.8.cloned.1.call-start = ((), (), s32[]{:S(2)}) async-start(), calls=%async_computation.1 | async-start | bytes 2097152 | tf_op jit(solution)/shard_map/psum | solution.py:21
  8.4 29.9 %collective-permute-start.5 = (bf16[1,2,128,1024]{3,2,1,0:T(8,128)(2,1)S(1)}, bf16[1,2,128,1024]{3,2,1,0:T(8,128)(2,1)}, u32[]{:S(2)}, u32[]{:S(2)}) collective-permute-start(bf16[1,2,128,1024]{3,2,1,0:T(8,128)(2,1)S(1)} %bitcast.327), channel_id=1, source_target_pairs={{12,0},{16,4},{20,8},{24,12},{28,16},{32,20},{36,24},{40,28},{44,3... | collective-permute-start | bytes 1572872 | tf_op jit(solution)/shard_map/ppermute | solution.py:16
  9.7 36.0 %collective-permute-start.4 = (bf16[1,2,128,1024]{3,2,1,0:T(8,128)(2,1)S(1)}, bf16[1,2,128,1024]{3,2,1,0:T(8,128)(2,1)}, u32[]{:S(2)}, u32[]{:S(2)}) collective-permute-start(bf16[1,2,128,1024]{3,2,1,0:T(8,128)(2,1)S(1)} %bitcast.328), channel_id=1, source_target_pairs={{8,0},{12,4},{16,8},{20,12},{24,16},{28,20},{32,24},{36,28},{40,32... | collective-permute-start | bytes 1572872 | tf_op jit(solution)/shard_map/ppermute | solution.py:16
  13.9 31.8 %collective-permute-start.3 = (bf16[1,2,128,1024]{3,2,1,0:T(8,128)(2,1)S(1)}, bf16[1,2,128,1024]{3,2,1,0:T(8,128)(2,1)}, u32[]{:S(2)}, u32[]{:S(2)}) collective-permute-start(bf16[1,2,128,1024]{3,2,1,0:T(8,128)(2,1)S(1)} %bitcast.329), channel_id=1, source_target_pairs={{4,0},{8,4},{12,8},{16,12},{20,16},{24,20},{28,24},{32,28},{36,32}... | collective-permute-start | bytes 1572872 | tf_op jit(solution)/shard_map/ppermute | solution.py:16
  15.9 32.3 %collective-permute-start.2 = (bf16[1,2,128,1024]{3,2,1,0:T(8,128)(2,1)S(1)}, bf16[1,2,128,1024]{3,2,1,0:T(8,128)(2,1)}, u32[]{:S(2)}, u32[]{:S(2)}) collective-permute-start(bf16[1,2,128,1024]{3,2,1,0:T(8,128)(2,1)S(1)} %bitcast.330), channel_id=1, source_target_pairs={{0,12},{4,16},{8,20},{12,24},{16,28},{20,32},{24,36},{28,40},{32,4... | collective-permute-start | bytes 1572872 | tf_op jit(solution)/shard_map/ppermute | solution.py:16
  20.7 28.1 %collective-permute-start.1 = (bf16[1,2,128,1024]{3,2,1,0:T(8,128)(2,1)S(1)}, bf16[1,2,128,1024]{3,2,1,0:T(8,128)(2,1)}, u32[]{:S(2)}, u32[]{:S(2)}) collective-permute-start(bf16[1,2,128,1024]{3,2,1,0:T(8,128)(2,1)S(1)} %bitcast.331), channel_id=1, source_target_pairs={{0,8},{4,12},{8,16},{12,20},{16,24},{20,28},{24,32},{28,36},{32,40... | collective-permute-start | bytes 1572872 | tf_op jit(solution)/shard_map/ppermute | solution.py:16
  25.0 541.6 %all-reduce.6.cloned.1.call-start = ((), (), s32[]{:S(2)}) async-start(), calls=%async_computation | async-start | bytes 2097152 | tf_op jit(solution)/shard_map/psum | solution.py:181
  32.8 22.8 %copy-start.25 = (pred[2,4,14]{2,1,0:T(4,128)(4,1)}, pred[2,4,14]{2,1,0:T(4,128)(4,1)S(1)}, u32[]{:S(2)}) copy-start(pred[2,4,14]{2,1,0:T(4,128)(4,1)S(1)} %broadcast_compare_fusion.2) | copy-start | bytes 340
  38.1 208.3 %copy-start.9 = (bf16[1,1,128,4,8,128]{5,4,3,2,1,0:T(8,128)(2,1)}, bf16[1,1,128,4,8,128]{5,4,3,2,1,0:T(8,128)(2,1)S(1)}, u32[]{:S(2)}) copy-start(bf16[1,1,128,4,8,128]{5,4,3,2,1,0:T(8,128)(2,1)S(1)} %get-tuple-element.29) | copy-start | bytes 3145732
  38.3 15.0 %collective-permute-start = (bf16[1,2,128,1024]{3,2,1,0:T(8,128)(2,1)S(1)}, bf16[1,2,128,1024]{3,2,1,0:T(8,128)(2,1)S(1)}, u32[]{:S(2)}, u32[]{:S(2)}) collective-permute-start(bf16[1,2,128,1024]{3,2,1,0:T(8,128)(2,1)S(1)} %bitcast.333), channel_id=1, source_target_pairs={{0,4},{4,8},{8,12},{12,16},{16,20},{20,24},{24,28},{28,32},{32,36}... | collective-permute-start | bytes 1572872 | tf_op jit(solution)/shard_map/ppermute | solution.py:16
  239.1 9.7 %copy-start.5 = (bf16[768,4,128]{2,1,0:T(4,128)(2,1)}, bf16[768,4,128]{2,1,0:T(4,128)(2,1)S(1)}, u32[]{:S(2)}) copy-start(bf16[768,4,128]{2,1,0:T(4,128)(2,1)S(1)} %reshape.1055) | copy-start | bytes 2359300
  252.0 5.3 copy-start.24
  262.6 7.1 %copy-start.15 = (f32[1,768,4,128]{3,1,2,0:T(8,128)S(1)}, f32[1,768,4,128]{3,1,2,0:T(8,128)}, u32[]{:S(2)}) copy-start(f32[1,768,4,128]{3,1,2,0:T(8,128)} %fusion.40) | copy-start | bytes 4718596
  262.6 10.2 %copy-start.10 = (bf16[1,1,128,4,8,128]{5,4,3,2,1,0:T(8,128)(2,1)S(1)}, bf16[1,1,128,4,8,128]{5,4,3,2,1,0:T(8,128)(2,1)}, u32[]{:S(2)}) copy-start(bf16[1,1,128,4,8,128]{5,4,3,2,1,0:T(8,128)(2,1)} %copy-done.9) | copy-start | bytes 3145732
  276.2 6.6 %copy-start.7 = (bf16[1,1,128,4,8,128]{5,4,3,2,1,0:T(8,128)(2,1)S(1)}, bf16[1,1,128,4,8,128]{5,4,3,2,1,0:T(8,128)(2,1)}, u32[]{:S(2)}) copy-start(bf16[1,1,128,4,8,128]{5,4,3,2,1,0:T(8,128)(2,1)} %get-tuple-element.28) | copy-start | bytes 3145732
  298.3 7.3 %copy-start.16 = (f32[1,768,4,128]{3,1,2,0:T(8,128)S(1)}, f32[1,768,4,128]{3,1,2,0:T(8,128)}, u32[]{:S(2)}) copy-start(f32[1,768,4,128]{3,1,2,0:T(8,128)} %fusion.37) | copy-start | bytes 4718596
  298.4 10.5 %copy-start.8 = (bf16[1,1,128,4,8,128]{5,4,3,2,1,0:T(8,128)(2,1)S(1)}, bf16[1,1,128,4,8,128]{5,4,3,2,1,0:T(8,128)(2,1)}, u32[]{:S(2)}) copy-start(bf16[1,1,128,4,8,128]{5,4,3,2,1,0:T(8,128)(2,1)} %get-tuple-element.28) | copy-start | bytes 3145732
  312.2 6.0 %copy-start.26 = (pred[2,4,14]{2,1,0:T(4,128)(4,1)S(1)}, pred[2,4,14]{2,1,0:T(4,128)(4,1)}, u32[]{:S(2)}) copy-start(pred[2,4,14]{2,1,0:T(4,128)(4,1)} %copy-done.25) | copy-start | bytes 340
  318.2 6.9 %copy-start.3 = (f32[1,6,128,1024]{3,1,2,0:T(8,128)S(1)}, f32[1,6,128,1024]{3,1,2,0:T(8,128)}, u32[]{:S(2)}) copy-start(f32[1,6,128,1024]{3,1,2,0:T(8,128)} %copy_dynamic-update-slice_fusion.1) | copy-start | bytes 9437188
  318.2 6.9 %copy-start.11 = (f32[1,768,4,128]{3,2,0,1:T(4,128)S(1)}, f32[1,768,4,128]{3,2,0,1:T(4,128)}, u32[]{:S(2)}) copy-start(f32[1,768,4,128]{3,2,0,1:T(4,128)} %copy.107) | copy-start | bytes 4718596
  328.1 31.9 %slice-start = ((s8[6291456]{0:T(1024)(128)(4,1)}), s8[2097152]{0:T(1024)(128)(4,1)S(1)}, s32[]{:S(2)}) async-start(s8[6291456]{0:T(1024)(128)(4,1)} %bitcast.308), calls=%async_computation.2 | async-start | bytes 4194304
  330.1 29.8 %slice-start.1 = ((s8[6291456]{0:T(1024)(128)(4,1)}), s8[4194304]{0:T(1024)(128)(4,1)S(1)}, s32[]{:S(2)}) async-start(s8[6291456]{0:T(1024)(128)(4,1)} %bitcast.308), calls=%async_computation.3 | async-start | bytes 8388608
  340.8 19.2 %copy-start.6 = (bf16[768,4,128]{2,1,0:T(4,128)(2,1)S(1)}, bf16[768,4,128]{2,1,0:T(4,128)(2,1)}, u32[]{:S(2)}) copy-start(bf16[768,4,128]{2,1,0:T(4,128)(2,1)} %copy-done.5) | copy-start | bytes 2359300
  345.6 43.2 %collective-permute-start.7 = (f32[1,2,128,1024]{3,1,2,0:T(2,128)S(1)}, f32[1,2,128,1024]{3,1,2,0:T(2,128)S(1)}, u32[]{:S(2)}, u32[]{:S(2)}) collective-permute-start(f32[1,2,128,1024]{3,1,2,0:T(2,128)S(1)} %get-tuple-element.20), channel_id=1, source_target_pairs={{8,0},{12,4},{16,8},{20,12},{24,16},{28,20},{32,24},{36,28},{40,32... | collective-permute-start | bytes 3145736 | tf_op jit(solution)/shard_map/ppermute | solution.py:16
  348.1 221.1 %collective-permute-start.11 = (f32[1,2,128,1024]{3,1,2,0:T(2,128)}, f32[1,2,128,1024]{3,1,2,0:T(2,128)}, u32[]{:S(2)}, u32[]{:S(2)}) collective-permute-start(f32[1,2,128,1024]{3,1,2,0:T(2,128)} %get-tuple-element.21), channel_id=1, source_target_pairs={{0,12},{4,16},{8,20},{12,24},{16,28},{20,32},{24,36},{28,40},{32,4... | collective-permute-start | bytes 3145736 | tf_op jit(solution)/shard_map/ppermute | solution.py:16
  350.4 218.7 %collective-permute-start.10 = (f32[1,2,128,1024]{3,1,2,0:T(2,128)}, f32[1,2,128,1024]{3,1,2,0:T(2,128)}, u32[]{:S(2)}, u32[]{:S(2)}) collective-permute-start(f32[1,2,128,1024]{3,1,2,0:T(2,128)} %get-tuple-element.22), channel_id=1, source_target_pairs={{0,8},{4,12},{8,16},{12,20},{16,24},{20,28},{24,32},{28,36},{32,40... | collective-permute-start | bytes 3145736 | tf_op jit(solution)/shard_map/ppermute | solution.py:16
  353.4 215.8 %collective-permute-start.9 = (f32[1,2,128,1024]{3,1,2,0:T(2,128)}, f32[1,2,128,1024]{3,1,2,0:T(2,128)}, u32[]{:S(2)}, u32[]{:S(2)}) collective-permute-start(f32[1,2,128,1024]{3,1,2,0:T(2,128)} %get-tuple-element.23), channel_id=1, source_target_pairs={{0,4},{4,8},{8,12},{12,16},{16,20},{20,24},{24,28},{28,32},{32,36}... | collective-permute-start | bytes 3145736 | tf_op jit(solution)/shard_map/ppermute | solution.py:16
  357.9 211.2 %collective-permute-start.8 = (f32[1,2,128,1024]{3,1,2,0:T(2,128)}, f32[1,2,128,1024]{3,1,2,0:T(2,128)}, u32[]{:S(2)}, u32[]{:S(2)}) collective-permute-start(f32[1,2,128,1024]{3,1,2,0:T(2,128)} %get-tuple-element.24), channel_id=1, source_target_pairs={{12,0},{16,4},{20,8},{24,12},{28,16},{32,20},{36,24},{40,28},{44,3... | collective-permute-start | bytes 3145736 | tf_op jit(solution)/shard_map/ppermute | solution.py:16
  388.9 180.3 %collective-permute-start.6 = (f32[1,2,128,1024]{3,1,2,0:T(2,128)}, f32[1,2,128,1024]{3,1,2,0:T(2,128)}, u32[]{:S(2)}, u32[]{:S(2)}) collective-permute-start(f32[1,2,128,1024]{3,1,2,0:T(2,128)} %get-tuple-element.25), channel_id=1, source_target_pairs={{4,0},{8,4},{12,8},{16,12},{20,16},{24,20},{28,24},{32,28},{36,32}... | collective-permute-start | bytes 3145736 | tf_op jit(solution)/shard_map/ppermute | solution.py:16
  391.1 175.4 %copy-start.27 = (f32[2]{0:T(128)S(1)}, f32[2]{0:T(128)}, u32[]{:S(2)}) copy-start(f32[2]{0:T(128)} %compare_convert_fusion) | copy-start | bytes 28
  392.7 176.5 %copy-start.22 = (f32[1,2,128,1024]{3,1,2,0:T(2,128)S(1)}, f32[1,2,128,1024]{3,1,2,0:T(2,128)}, u32[]{:S(2)}) copy-start(f32[1,2,128,1024]{3,1,2,0:T(2,128)} %copy-done.21) | copy-start | bytes 3145732
  (14 other events, 55.1 us)
Sparse Core Ops, SparseCore 0:
  25.1 197.4 all-reduce.7
  330.3 236.2 all-reduce.5
where the time goes:
time: 595 us; the launch traced here: 588 us
  waiting for transfers between devices  267 us (45%)
  blocking collectives  95.3 us (16%)
  matrix products  71.3 us (12%)
  local copies, waits for them, and re-layouts  70.5 us (12%)
  other arithmetic  34.4 us (6%)
  starting transfers between devices  34.1 us (6%)
  between operations  15.7 us (3%)
    psum x1, waiting for transfers between devices, broadcast(): return lax.psum(kept, axis)  163 us
    psum x1, blocking collectives, body(): bias_total = lax.psum(local_bias, ('ctx', 'dp'))  95.3 us
    psum x1, waiting for transfers between devices, body(): shared_total = lax.psum(prompt_grad, 'ctx')  75.6 us
    ppermute x12, starting transfers between devices, from_behind(): lax.ppermute(value, axis, [(source, source + steps) for source in range(i...  34 us
    ppermute x12, waiting for transfers between devices, from_behind(): lax.ppermute(value, axis, [(source, source + steps) for source in range(i...  28.9 us
    dot_general x2, matrix products, body(): jnp.einsum('dn,tdbf->tnbf', chooser[half_idx].astype(jnp.float32), contri...  17.5 us
    unnamed x69, local copies, waits for them, and re-layouts  14.9 us
    dot_general x2, matrix products, attend(): jnp.einsum('tqkgd,tskd->tkgqs', grad_rows, cand_vals, preferred_element_t...  14.4 us
  transfers between devices with their start and end apart: 14, of which 5 were waited for; matrix products, arithmetic and copies ran while one was open for 9% of the time, Pallas kernels for 0%

commit v1 on v0

--- a/solution.py
+++ b/solution.py
@@ -178,7 +178,7 @@
     owners = jnp.arange(PROMPT, dtype=jnp.int32)
     query_all = jnp.stack(query_parts, axis=1)
     local_bias = jnp.sum(query_all, axis=(0, 1, 2)).reshape(width_q)
-    shared_total = lax.psum(prompt_grad, "ctx")
+    shared_total = jnp.sum(lax.all_gather(prompt_grad, "ctx"), axis=0)
     bias_total = lax.psum(local_bias, ("ctx", "dp"))
     owned = (owners == rank_ctx).astype(jnp.float32)
     kv_grad = kv_grad.at[:, 0].add(jnp.sum(owned[None, :, None, None] * shared_total, axis=1))

time: 595 us -> 661 us (1.11)
  the two profiles are of different devices: /device:TPU:2 before, /device:TPU:1 now
where the time goes in v1:
time: 661 us; the launch traced here: 654 us
  waiting for transfers between devices  289 us (44%)
  blocking collectives  121 us (18%)
  matrix products  69.8 us (11%)
  local copies, waits for them, and re-layouts  67.3 us (10%)
  other arithmetic  54.7 us (8%)
  starting transfers between devices  37.4 us (6%)
  between operations  15.8 us (2%)
    psum x1, waiting for transfers between devices, broadcast(): return lax.psum(kept, axis)  161 us
    psum x1, blocking collectives, body(): bias_total = lax.psum(local_bias, ('ctx', 'dp'))  121 us
    all_gather x1, waiting for transfers between devices, body(): shared_total = jnp.sum(lax.all_gather(prompt_grad, 'ctx'), axis=0)  98.3 us
    ppermute x12, starting transfers between devices, from_behind(): lax.ppermute(value, axis, [(source, source + steps) for source in range(i...  37.3 us
    ppermute x12, waiting for transfers between devices, from_behind(): lax.ppermute(value, axis, [(source, source + steps) for source in range(i...  29.7 us
    reduce_sum x1, other arithmetic, body(): shared_total = jnp.sum(lax.all_gather(prompt_grad, 'ctx'), axis=0)  20.8 us
    unnamed x61, local copies, waits for them, and re-layouts  15.4 us
    dot_general x2, matrix products, attend(): jnp.einsum('tqkgd,tskd->tkgqs', grad_rows, cand_vals, preferred_element_t...  14.1 us
  transfers between devices with their start and end apart: 14, of which 7 were waited for; matrix products, arithmetic and copies ran while one was open for 9% of the time, Pallas kernels for 0%

profile of v1, /device:TPU:1, one launch (start us, length us, event | category | flops | bytes accessed | tf_op | source)
XLA Modules:
  0.0 654.4 jit_solution(10345261271423391256)
XLA Ops:
  11.8 5.2 collective-permute-start.3
  17.0 7.4 %collective-permute-start.2 = (bf16[1,2,128,1024]{3,2,1,0:T(8,128)(2,1)}, bf16[1,2,128,1024]{3,2,1,0:T(8,128)(2,1)}, u32[]{:S(2)}, u32[]{:S(2)}) collective-permute-start(bf16[1,2,128,1024]{3,2,1,0:T(8,128)(2,1)} %bitcast), channel_id=1, source_target_pairs={{0,12},{4,16},{8,20},{12,24},{16,28},{20,32},{24,36},{28,40},{32,4... | collective-permute-start | bytes 1572872 | tf_op jit(solution)/shard_map/ppermute | solution.py:16
  24.4 2.8 collective-permute-start.1
  48.6 5.9 collective-permute-done
  56.7 2.9 convert_bitcast_fusion
  61.7 160.8 %all-reduce.5.cloned.1.call-done = (bf16[1,1,128,1024]{3,1,2,0:T(2,128)(2,1)}, bf16[1,1,128,1024]{3,1,2,0:T(2,128)(2,1)}) async-done(((bf16[1,1,128,1024]{3,1,2,0:T(2,128)(2,1)}, bf16[1,1,128,1024]{3,1,2,0:T(2,128)(2,1)}), (bf16[1,1,128,1024]{3,1,2,0:T(2,128)(2,1)}, bf16[1,1,128,1024]{3,1,2,0:T(2,128)(2,1)})) %all-reduce.5.cloned.1.call-update) | async-done | bytes 524304 | tf_op jit(solution)/shard_map/psum | solution.py:21
  222.4 4.8 pad_maximum_fusion
  238.4 3.2 fusion.9
  241.7 4.9 fusion.40
  246.5 5.3 fusion.29
  251.9 7.1 %fusion.11 = bf16[4,8,128,768]{2,3,1,0:T(8,128)(2,1)} fusion(f32[4,8,128]{2,1,0:T(8,128)S(1)} %bitcast.332, f32[4,8,128]{2,1,0:T(8,128)S(1)} %broadcast_select_fusion.2, f32[4,8,128]{2,1,0:T(8,128)S(1)} %get-tuple-element.46, f32[4,768,128,8]{2,1,3,0:T(8,128)S(1)} %get-tuple-element.47, pred[128,768]{0,1:T(8,128)(4,1)S(1)} %and_and_fusion, ...), kind=kOutput, calls=%fused_computation.19 | convolution fusion | flops 830472192 | bytes 20856832 | tf_op jit(solution)/shard_map/tqkgd,tskd->tkgqs/dot_general | solution.py:41
  268.5 3.1 fusion.7
  271.7 5.0 fusion.37
  276.7 5.2 fusion.30
  281.9 7.0 %fusion.10 = bf16[4,8,128,768]{2,3,1,0:T(8,128)(2,1)S(1)} fusion(f32[4,8,128]{2,1,0:T(8,128)S(1)} %bitcast.333, f32[4,8,128]{2,1,0:T(8,128)S(1)} %broadcast_select_fusion.3, f32[4,8,128]{2,1,0:T(8,128)S(1)} %get-tuple-element.48, f32[4,768,128,8]{2,1,3,0:T(8,128)S(1)} %get-tuple-element.49, pred[128,768]{0,1:T(8,128)(4,1)S(1)} %and_and_fusion.1, ...), kind=kOutput, calls=%fused_computation.18 | convolution fusion | flops 830472192 | bytes 20856832 | tf_op jit(solution)/shard_map/tqkgd,tskd->tkgqs/dot_general | solution.py:41
  291.5 3.4 fusion.36
  294.9 3.1 copy.144
  298.0 3.7 copy_dynamic-update-slice_fusion.3
  301.8 3.6 copy.145
  305.3 6.1 fusion.35
  311.5 2.6 copy.150
  325.5 7.5 %fusion.28 = f32[128,1024,14]{1,2,0:T(8,128)S(1)} fusion(f32[1,6,128,1024]{3,1,2,0:T(8,128)} %copy-done.3, pred[2,4,14]{2,1,0:T(4,128)(4,1)S(1)} %copy-done.23), kind=kOutput, calls=%fused_computation.40 | convolution fusion | flops 88080384 | bytes 9437696 | tf_op jit(solution)/shard_map/dn,tdbf->tnbf/dot_general | solution.py:154
  333.0 5.9 add_bitcast_fusion
  338.9 3.5 fusion.72
  343.4 6.9 %collective-permute-start.11 = (f32[1,2,128,1024]{3,1,2,0:T(2,128)S(1)}, f32[1,2,128,1024]{3,1,2,0:T(2,128)S(1)}, u32[]{:S(2)}, u32[]{:S(2)}) collective-permute-start(f32[1,2,128,1024]{3,1,2,0:T(2,128)S(1)} %get-tuple-element.21), channel_id=1, source_target_pairs={{0,12},{4,16},{8,20},{12,24},{16,28},{20,32},{24,36},{28,40},{32,4... | collective-permute-start | bytes 3145736 | tf_op jit(solution)/shard_map/ppermute | solution.py:16
  356.1 3.4 collective-permute-start.6
  364.4 21.4 %collective-permute-done.11 = f32[1,2,128,1024]{3,1,2,0:T(2,128)S(1)} collective-permute-done((f32[1,2,128,1024]{3,1,2,0:T(2,128)S(1)}, f32[1,2,128,1024]{3,1,2,0:T(2,128)S(1)}, u32[]{:S(2)}, u32[]{:S(2)}) %collective-permute-start.11) | collective-permute-done | bytes 1048608 | tf_op jit(solution)/shard_map/ppermute | solution.py:16
  391.8 120.7 %psum.23 = f32[4096]{0:T(1024)S(1)} all-reduce(f32[4096]{0:T(1024)S(1)} %add_bitcast_fusion.1), channel_id=1, replica_groups=mesh['ctx'=64,'dp'=4] {'ctx','dp'}, use_global_device_ids=true, to_apply=%region_14.15 | all-reduce | flops 4096 | bytes 32768 | tf_op jit(solution)/shard_map/psum | solution.py:182
  513.2 6.1 fusion.45
  519.3 98.3 %all-gather.3.cloned.1.call-done = f32[64,2,128,1024]{3,2,1,0:T(8,128)} async-done(((f32[1,2,128,1024]{3,2,1,0:T(8,128)}), f32[64,2,128,1024]{3,2,1,0:T(8,128)}) %all-gather.3.cloned.1.call-update) | async-done | bytes 67108880 | tf_op jit(solution)/shard_map/all_gather | solution.py:181
  617.6 20.8 %reduce.17 = f32[2,128,1024]{2,1,0:T(8,128)S(1)} reduce(f32[64,2,128,1024]{3,2,1,0:T(8,128)} %all-gather.3.cloned.1.call-done, f32[]{:T(128)} %constant.84.clone.1), dimensions={0}, to_apply=%region_10.11 | reduce | flops 16515072 | bytes 68157440 | tf_op jit(solution)/shard_map/reduce_sum | solution.py:181
  641.4 3.7 scatter-add.4
  (164 shorter events, 87.4 us)
Async XLA Ops:
  7.2 26.6 %copy-start.12 = (bf16[1,256,4096]{2,1,0:T(8,128)(2,1)S(1)}, bf16[1,256,4096]{2,1,0:T(8,128)(2,1)}, u32[]{:S(2)}) copy-start(bf16[1,256,4096]{2,1,0:T(8,128)(2,1)} %param.9) | copy-start | bytes 6291460
  7.2 215.2 %all-reduce.5.cloned.1.call-start = ((), (), s32[]{:S(2)}) async-start(), calls=%async_computation.1 | async-start | bytes 2097152 | tf_op jit(solution)/shard_map/psum | solution.py:21
  9.2 31.9 %collective-permute-start.5 = (bf16[1,2,128,1024]{3,2,1,0:T(8,128)(2,1)}, bf16[1,2,128,1024]{3,2,1,0:T(8,128)(2,1)S(1)}, u32[]{:S(2)}, u32[]{:S(2)}) collective-permute-start(bf16[1,2,128,1024]{3,2,1,0:T(8,128)(2,1)} %bitcast), channel_id=1, source_target_pairs={{12,0},{16,4},{20,8},{24,12},{28,16},{32,20},{36,24},{40,28},{44,3... | collective-permute-start | bytes 1572872 | tf_op jit(solution)/shard_map/ppermute | solution.py:16
  10.5 33.6 %collective-permute-start.4 = (bf16[1,2,128,1024]{3,2,1,0:T(8,128)(2,1)}, bf16[1,2,128,1024]{3,2,1,0:T(8,128)(2,1)}, u32[]{:S(2)}, u32[]{:S(2)}) collective-permute-start(bf16[1,2,128,1024]{3,2,1,0:T(8,128)(2,1)} %bitcast), channel_id=1, source_target_pairs={{8,0},{12,4},{16,8},{20,12},{24,16},{28,20},{32,24},{36,28},{40,32... | collective-permute-start | bytes 1572872 | tf_op jit(solution)/shard_map/ppermute | solution.py:16
  11.8 34.2 %collective-permute-start.3 = (bf16[1,2,128,1024]{3,2,1,0:T(8,128)(2,1)}, bf16[1,2,128,1024]{3,2,1,0:T(8,128)(2,1)}, u32[]{:S(2)}, u32[]{:S(2)}) collective-permute-start(bf16[1,2,128,1024]{3,2,1,0:T(8,128)(2,1)} %bitcast), channel_id=1, source_target_pairs={{4,0},{8,4},{12,8},{16,12},{20,16},{24,20},{28,24},{32,28},{36,32}... | collective-permute-start | bytes 1572872 | tf_op jit(solution)/shard_map/ppermute | solution.py:16
  17.0 31.5 %collective-permute-start.2 = (bf16[1,2,128,1024]{3,2,1,0:T(8,128)(2,1)}, bf16[1,2,128,1024]{3,2,1,0:T(8,128)(2,1)}, u32[]{:S(2)}, u32[]{:S(2)}) collective-permute-start(bf16[1,2,128,1024]{3,2,1,0:T(8,128)(2,1)} %bitcast), channel_id=1, source_target_pairs={{0,12},{4,16},{8,20},{12,24},{16,28},{20,32},{24,36},{28,40},{32,4... | collective-permute-start | bytes 1572872 | tf_op jit(solution)/shard_map/ppermute | solution.py:16
  24.4 24.2 %collective-permute-start.1 = (bf16[1,2,128,1024]{3,2,1,0:T(8,128)(2,1)}, bf16[1,2,128,1024]{3,2,1,0:T(8,128)(2,1)}, u32[]{:S(2)}, u32[]{:S(2)}) collective-permute-start(bf16[1,2,128,1024]{3,2,1,0:T(8,128)(2,1)} %bitcast), channel_id=1, source_target_pairs={{0,8},{4,12},{8,16},{12,20},{16,24},{20,28},{24,32},{28,36},{32,40... | collective-permute-start | bytes 1572872 | tf_op jit(solution)/shard_map/ppermute | solution.py:16
  28.7 10.4 %copy-start.13 = (bf16[1,2,128,1024]{3,1,2,0:T(2,128)(2,1)}, bf16[1,2,128,1024]{3,1,2,0:T(2,128)(2,1)S(1)}, u32[]{:S(2)}) copy-start(bf16[1,2,128,1024]{3,1,2,0:T(2,128)(2,1)S(1)} %copy.114) | copy-start | bytes 1572868
  30.5 587.1 %all-gather.3.cloned.1.call-start = ((), (), s32[]{:S(2)}) async-start(), calls=%async_computation | async-start | bytes 68157440 | tf_op jit(solution)/shard_map/all_gather | solution.py:181
  36.6 20.1 %copy-start.22 = (pred[2,4,14]{2,1,0:T(4,128)(4,1)}, pred[2,4,14]{2,1,0:T(4,128)(4,1)S(1)}, u32[]{:S(2)}) copy-start(pred[2,4,14]{2,1,0:T(4,128)(4,1)S(1)} %broadcast_compare_fusion.2) | copy-start | bytes 340
  41.2 13.3 %collective-permute-start = (bf16[1,2,128,1024]{3,2,1,0:T(8,128)(2,1)}, bf16[1,2,128,1024]{3,2,1,0:T(8,128)(2,1)S(1)}, u32[]{:S(2)}, u32[]{:S(2)}) collective-permute-start(bf16[1,2,128,1024]{3,2,1,0:T(8,128)(2,1)} %bitcast), channel_id=1, source_target_pairs={{0,4},{4,8},{8,12},{12,16},{16,20},{20,24},{24,28},{28,32},{32,36}... | collective-permute-start | bytes 1572872 | tf_op jit(solution)/shard_map/ppermute | solution.py:16
  43.7 192.3 %copy-start.8 = (bf16[1,1,128,4,8,128]{5,4,3,2,1,0:T(8,128)(2,1)}, bf16[1,1,128,4,8,128]{5,4,3,2,1,0:T(8,128)(2,1)S(1)}, u32[]{:S(2)}) copy-start(bf16[1,1,128,4,8,128]{5,4,3,2,1,0:T(8,128)(2,1)S(1)} %get-tuple-element.29) | copy-start | bytes 3145732
  46.0 10.7 %copy-start.14 = (bf16[1,2,128,1024]{3,1,2,0:T(2,128)(2,1)S(1)}, bf16[1,2,128,1024]{3,1,2,0:T(2,128)(2,1)}, u32[]{:S(2)}) copy-start(bf16[1,2,128,1024]{3,1,2,0:T(2,128)(2,1)} %copy-done.13) | copy-start | bytes 1572868
  251.8 7.1 %copy-start.10 = (bf16[1,6,128,1024]{3,1,2,0:T(8,128)(2,1)S(1)}, bf16[1,6,128,1024]{3,1,2,0:T(8,128)(2,1)}, u32[]{:S(2)}) copy-start(bf16[1,6,128,1024]{3,1,2,0:T(8,128)(2,1)} %get-tuple-element.36) | copy-start | bytes 4718596
  271.7 5.0 copy-start.19
  276.7 5.2 copy-start.16
  294.9 10.4 %copy-start.9 = (bf16[1,1,128,4,8,128]{5,4,3,2,1,0:T(8,128)(2,1)S(1)}, bf16[1,1,128,4,8,128]{5,4,3,2,1,0:T(8,128)(2,1)}, u32[]{:S(2)}) copy-start(bf16[1,1,128,4,8,128]{5,4,3,2,1,0:T(8,128)(2,1)} %copy-done.8) | copy-start | bytes 3145732
  314.1 4.9 copy-start.2
  314.1 4.9 copy-start.11
  319.1 6.4 copy-start.23
  325.5 7.5 %copy-start.5 = (f32[1,6,128,1024]{3,1,2,0:T(8,128)S(1)}, f32[1,6,128,1024]{3,1,2,0:T(8,128)}, u32[]{:S(2)}) copy-start(f32[1,6,128,1024]{3,1,2,0:T(8,128)} %copy-done.4) | copy-start | bytes 9437188
  325.5 34.0 %slice-start = ((s8[6291456]{0:T(1024)(128)(4,1)}), s8[4194304]{0:T(1024)(128)(4,1)S(1)}, s32[]{:S(2)}) async-start(s8[6291456]{0:T(1024)(128)(4,1)} %bitcast.308), calls=%async_computation.2 | async-start | bytes 8388608
  333.0 26.5 %slice-start.1 = ((s8[6291456]{0:T(1024)(128)(4,1)}), s8[2097152]{0:T(1024)(128)(4,1)S(1)}, s32[]{:S(2)}) async-start(s8[6291456]{0:T(1024)(128)(4,1)} %bitcast.308), calls=%async_computation.3 | async-start | bytes 4194304
  338.9 20.6 %copy-start.7 = (bf16[768,4,128]{2,1,0:T(4,128)(2,1)S(1)}, bf16[768,4,128]{2,1,0:T(4,128)(2,1)}, u32[]{:S(2)}) copy-start(bf16[768,4,128]{2,1,0:T(4,128)(2,1)} %copy-done.6) | copy-start | bytes 2359300
  343.4 42.4 %collective-permute-start.11 = (f32[1,2,128,1024]{3,1,2,0:T(2,128)S(1)}, f32[1,2,128,1024]{3,1,2,0:T(2,128)S(1)}, u32[]{:S(2)}, u32[]{:S(2)}) collective-permute-start(f32[1,2,128,1024]{3,1,2,0:T(2,128)S(1)} %get-tuple-element.21), channel_id=1, source_target_pairs={{0,12},{4,16},{8,20},{12,24},{16,28},{20,32},{24,36},{28,40},{32,4... | collective-permute-start | bytes 3145736 | tf_op jit(solution)/shard_map/ppermute | solution.py:16
  350.3 162.8 %collective-permute-start.9 = (f32[1,2,128,1024]{3,1,2,0:T(2,128)}, f32[1,2,128,1024]{3,1,2,0:T(2,128)}, u32[]{:S(2)}, u32[]{:S(2)}) collective-permute-start(f32[1,2,128,1024]{3,1,2,0:T(2,128)} %get-tuple-element.23), channel_id=1, source_target_pairs={{0,4},{4,8},{8,12},{12,16},{16,20},{20,24},{24,28},{28,32},{32,36}... | collective-permute-start | bytes 3145736 | tf_op jit(solution)/shard_map/ppermute | solution.py:16
  352.3 160.9 %collective-permute-start.10 = (f32[1,2,128,1024]{3,1,2,0:T(2,128)}, f32[1,2,128,1024]{3,1,2,0:T(2,128)}, u32[]{:S(2)}, u32[]{:S(2)}) collective-permute-start(f32[1,2,128,1024]{3,1,2,0:T(2,128)} %get-tuple-element.22), channel_id=1, source_target_pairs={{0,8},{4,12},{8,16},{12,20},{16,24},{20,28},{24,32},{28,36},{32,40... | collective-permute-start | bytes 3145736 | tf_op jit(solution)/shard_map/ppermute | solution.py:16
  354.8 158.4 %collective-permute-start.8 = (f32[1,2,128,1024]{3,1,2,0:T(2,128)}, f32[1,2,128,1024]{3,1,2,0:T(2,128)}, u32[]{:S(2)}, u32[]{:S(2)}) collective-permute-start(f32[1,2,128,1024]{3,1,2,0:T(2,128)} %get-tuple-element.24), channel_id=1, source_target_pairs={{12,0},{16,4},{20,8},{24,12},{28,16},{32,20},{36,24},{40,28},{44,3... | collective-permute-start | bytes 3145736 | tf_op jit(solution)/shard_map/ppermute | solution.py:16
  356.1 5.9 slice-start.2
  356.1 5.9 slice-start.3
  356.1 157.1 %collective-permute-start.6 = (f32[1,2,128,1024]{3,1,2,0:T(2,128)}, f32[1,2,128,1024]{3,1,2,0:T(2,128)}, u32[]{:S(2)}, u32[]{:S(2)}) collective-permute-start(f32[1,2,128,1024]{3,1,2,0:T(2,128)} %get-tuple-element.25), channel_id=1, source_target_pairs={{4,0},{8,4},{12,8},{16,12},{20,16},{24,20},{28,24},{32,28},{36,32}... | collective-permute-start | bytes 3145736 | tf_op jit(solution)/shard_map/ppermute | solution.py:16
  385.9 127.3 %collective-permute-start.7 = (f32[1,2,128,1024]{3,1,2,0:T(2,128)S(1)}, f32[1,2,128,1024]{3,1,2,0:T(2,128)}, u32[]{:S(2)}, u32[]{:S(2)}) collective-permute-start(f32[1,2,128,1024]{3,1,2,0:T(2,128)S(1)} %get-tuple-element.20), channel_id=1, source_target_pairs={{8,0},{12,4},{16,8},{20,12},{24,16},{28,20},{32,24},{36,28},{40,32... | collective-permute-start | bytes 3145736 | tf_op jit(solution)/shard_map/ppermute | solution.py:16
  (10 other events, 29.4 us)
Sparse Core Ops, SparseCore 0:
  30.6 191.7 all-reduce.4
  325.6 291.9 all-gather.2
